TPU v7x, 32 devices: a whole 2x2x4 slice. The times are simulated.
32 devices in a mesh: dp: 16 (over z, y, x), edge: 2 (over core).
Axes of the slice: x: 2, y: 2, z: 4, core: 2. Of those that a mesh axis runs over, the one named last changes fastest.
Arguments:
- node_feat: float32 [16, 8, 1152], P('dp', 'edge'), may hold values from -6 to 6
- cotangent: float32 [16, 8, 1152], P('dp', 'edge'), may hold values from -6 to 6
- w_zero: float32 [384, 384], replicated, may hold values from -0.3125 to 0.3125
- w_one: float32 [2, 256, 256], replicated, may hold values from -0.25 to 0.25
- w_two: float32 [2, 128, 128], replicated, may hold values from -0.375 to 0.375
- edge_src: int32 [16, 256], P('dp', 'edge'), may hold values from 0 to 7
- edge_tgt: int32 [16, 256], P('dp', 'edge'), may hold values from 0 to 7
- counts: int32 [16, 2], P('dp', 'edge'), may hold values from 32 to 128, as said below
- wigner: float32 [16, 34, 256], P('dp', None, 'edge'), may hold values from -1 to 1, as said below
- radial: float32 [16, 256, 128], P('dp', 'edge'), may hold values from 0.3 to 3
Outputs:
- aggregate: float32 [16, 8, 1152], P('dp', 'edge')
- feat_grad: float32 [16, 8, 1152], P('dp', 'edge')
- grad_zero: float32 [384, 384], P('edge')
- grad_one: float32 [2, 256, 256], P(None, 'edge')
- grad_two: float32 [2, 128, 128], P(None, 'edge')
Inputs may be any that keep to these rules, and one draw needn't show every extreme that they name: The first counts[g, d] edge slots of device d of batch g are used, the rest are padding; in every batch one device has all 128 slots used. `wigner`: for each edge the 9 degree-one entries and the 25 degree-two entries form the real Wigner matrices of one rotation, both orthogonal.
All inputs are finite; a program needn't handle non-finite values.
Results may differ from a plain program's by a relative error of at most 0.0003.
Values sent between devices are 32-bit elements; how exact they have to be, the bound alone decides.
A program may use at most 64 MiB of HBM per device.

v0:
```python
import math

import jax
import jax.numpy as jnp
from jax import lax
from jax.sharding import PartitionSpec as P

NEIGH = 32


PRECISE = lax.Precision.HIGHEST


def exact_dot(left, right):
    return jnp.dot(left, right, precision=PRECISE, preferred_element_type=jnp.float32)


def outer_sum(left, right):
    return jnp.einsum("ea,eb->ab", left, right, precision=PRECISE)


def rotate(wigner_cols, coeffs, inverse):
    edge_count = coeffs.shape[0]
    order_one = wigner_cols[0:9].reshape(3, 3, edge_count)
    order_two = wigner_cols[9:34].reshape(5, 5, edge_count)
    pattern = "jie,ejc->eic" if inverse else "ije,ejc->eic"
    part_one = jnp.einsum(pattern, order_one, coeffs[:, 1:4], precision=PRECISE)
    part_two = jnp.einsum(pattern, order_two, coeffs[:, 4:9], precision=PRECISE)
    return jnp.concatenate([coeffs[:, 0:1], part_one, part_two], axis=1)


def split_orders(coeffs):
    zero_part = jnp.concatenate([coeffs[:, 0], coeffs[:, 2], coeffs[:, 6]], axis=1)
    plus_one = jnp.concatenate([coeffs[:, 3], coeffs[:, 7]], axis=1)
    minus_one = jnp.concatenate([coeffs[:, 1], coeffs[:, 5]], axis=1)
    return (zero_part, plus_one, minus_one, coeffs[:, 8], coeffs[:, 4])


def join_orders(zero_part, plus_one, minus_one, plus_two, minus_two):
    channels = plus_two.shape[1]
    pieces = [
        zero_part[:, :channels],
        minus_one[:, :channels],
        zero_part[:, channels : 2 * channels],
        plus_one[:, :channels],
        minus_two,
        minus_one[:, channels:],
        zero_part[:, 2 * channels :],
        plus_one[:, channels:],
        plus_two,
    ]
    return jnp.stack(pieces, axis=1)


def mix_orders(rotated, weights_zero, weights_one, weights_two):
    zero_part, plus_one, minus_one, plus_two, minus_two = split_orders(rotated)
    return join_orders(
        exact_dot(zero_part, weights_zero),
        exact_dot(plus_one, weights_one[0]) - exact_dot(minus_one, weights_one[1]),
        exact_dot(minus_one, weights_one[0]) + exact_dot(plus_one, weights_one[1]),
        exact_dot(plus_two, weights_two[0]) - exact_dot(minus_two, weights_two[1]),
        exact_dot(minus_two, weights_two[0]) + exact_dot(plus_two, weights_two[1]),
    )


def mix_backward(rotated, grad_mixed, weights_zero, weights_one, weights_two):
    zero_part, plus_one, minus_one, plus_two, minus_two = split_orders(rotated)
    grad_zpart, grad_plus_one, grad_minus_one, grad_plus_two, grad_minus_two = split_orders(
        grad_mixed
    )
    zero_term = outer_sum(zero_part, grad_zpart)
    one_term = jnp.stack(
        [
            outer_sum(plus_one, grad_plus_one) + outer_sum(minus_one, grad_minus_one),
            outer_sum(plus_one, grad_minus_one) - outer_sum(minus_one, grad_plus_one),
        ]
    )
    two_term = jnp.stack(
        [
            outer_sum(plus_two, grad_plus_two) + outer_sum(minus_two, grad_minus_two),
            outer_sum(plus_two, grad_minus_two) - outer_sum(minus_two, grad_plus_two),
        ]
    )
    grad_input = join_orders(
        exact_dot(grad_zpart, weights_zero.T),
        exact_dot(grad_plus_one, weights_one[0].T) + exact_dot(grad_minus_one, weights_one[1].T),
        exact_dot(grad_minus_one, weights_one[0].T) - exact_dot(grad_plus_one, weights_one[1].T),
        exact_dot(grad_plus_two, weights_two[0].T) + exact_dot(grad_minus_two, weights_two[1].T),
        exact_dot(grad_minus_two, weights_two[0].T) - exact_dot(grad_plus_two, weights_two[1].T),
    )
    return (grad_input, zero_term, one_term, two_term)


def spreader(values, atom_ids, row_count):
    row_ids = lax.iota(jnp.int32, row_count)
    one_hot = (row_ids[:, None] == atom_ids[None, :]).astype(jnp.float32)
    return exact_dot(one_hot, values)


def local(node_feat, cotangent, w_zero, w_one, w_two, edge_src, edge_tgt, counts, wigner, radial):
    atom_dev = node_feat.shape[1]
    edge_dev = radial.shape[1]
    channels = radial.shape[2]
    shards = lax.axis_size("edge")
    sources = edge_src[0]
    targets = edge_tgt[0]
    wigner_cols = wigner[0]
    radial_rows = radial[0]
    slot_index = lax.iota(jnp.int32, edge_dev)
    edge_weight = jnp.where(slot_index < counts[0, 0], 1.0, 0.0).astype(jnp.float32) / math.sqrt(
        NEIGH
    )
    feat_rows = node_feat[0]
    cot_rows = cotangent[0]
    pieces = (
        lax.all_gather(feat_rows, "edge", axis=0, tiled=True),
        lax.all_gather(cot_rows, "edge", axis=0, tiled=True),
    )
    row_count = pieces[0].shape[0]
    atom_ids = lax.iota(jnp.int32, row_count)
    from_sources = (sources[:, None] == atom_ids[None, :]).astype(jnp.float32)
    from_targets = (targets[:, None] == atom_ids[None, :]).astype(jnp.float32)
    edge_feat = exact_dot(from_sources, pieces[0])
    edge_cot = exact_dot(from_targets, pieces[1])
    edge_in = edge_feat.reshape(edge_dev, 9, channels) * radial_rows[:, None, :]
    rotated = rotate(wigner_cols, edge_in, False)
    mixed = mix_orders(rotated, w_zero, w_one, w_two)
    message = (rotate(wigner_cols, mixed, True) * edge_weight[:, None, None]).reshape(
        edge_dev, 9 * channels
    )
    summed = lax.psum_scatter(
        spreader(message, targets, atom_dev * lax.axis_size("edge")),
        "edge",
        scatter_dimension=0,
        tiled=True,
    )
    grad_message = edge_cot.reshape(edge_dev, 9, channels) * edge_weight[:, None, None]
    grad_mixed = rotate(wigner_cols, grad_message, False)
    grad_rotated, zero_term, one_term, two_term = mix_backward(
        rotated, grad_mixed, w_zero, w_one, w_two
    )
    grad_edge = (rotate(wigner_cols, grad_rotated, True) * radial_rows[:, None, :]).reshape(
        edge_dev, 9 * channels
    )
    grad_rows = lax.psum_scatter(
        spreader(grad_edge, sources, atom_dev * lax.axis_size("edge")),
        "edge",
        scatter_dimension=0,
        tiled=True,
    )
    grad_scale = 1.0 / math.sqrt(lax.axis_size("dp") * shards * edge_dev)
    full_zero, full_one, full_two = lax.psum((zero_term, one_term, two_term), ("dp", "edge"))
    own = lax.axis_index("edge")
    size_zero = full_zero.shape[0] // shards
    size_one = full_one.shape[1] // shards
    size_two = full_two.shape[1] // shards
    rows_zero = lax.dynamic_slice_in_dim(full_zero, own * size_zero, size_zero, 0)
    rows_one = lax.dynamic_slice_in_dim(full_one, own * size_one, size_one, 1)
    rows_two = lax.dynamic_slice_in_dim(full_two, own * size_two, size_two, 1)
    return (
        summed[None],
        grad_rows[None],
        rows_zero * grad_scale,
        rows_one * grad_scale,
        rows_two * grad_scale,
    )


def solution(mesh):
    placed = (
        P("dp", "edge", None),
        P("dp", "edge", None),
        P(),
        P(),
        P(),
        P("dp", "edge"),
        P("dp", "edge"),
        P("dp", "edge"),
        P("dp", None, "edge"),
        P("dp", "edge", None),
    )
    return jax.shard_map(
        local,
        mesh=mesh,
        in_specs=placed,
        out_specs=(
            P("dp", "edge", None),
            P("dp", "edge", None),
            P("edge", None),
            P(None, "edge", None),
            P(None, "edge", None),
        ),
        check_vma=False,
    )
```

profile of v0, /device:TPU:0, one launch (start us, length us, event | category | flops | bytes accessed | tf_op | source)
XLA Modules:
  0.0 220.1 jit_solution(12185748471210908717)
XLA Ops:
  10.5 1.9 all-gather.1
  16.1 1.0 fusion.12
  18.0 0.9 fusion.59
  18.9 0.9 fusion.57
  20.7 1.0 fusion.18
  21.9 1.1 copy-done.1
  28.8 2.0 all-gather
  32.1 1.4 copy.55
  33.5 1.0 pad_maximum_fusion.5
  34.5 1.1 convolution_bitcast_fusion.2
  35.9 1.1 convolution_bitcast_fusion
  37.5 1.0 fusion.14
  38.5 1.0 fusion.20
  42.9 1.1 convolution_bitcast_fusion.3
  44.4 1.1 convolution_bitcast_fusion.1
  45.8 1.1 copy.65
  47.0 1.1 bitcast_multiply_fusion
  48.1 1.0 fusion.85
  49.4 1.0 fusion.86
  53.8 1.5 fusion.44
  60.7 10.2 %all-reduce.9.cloned.1.call-done = (f32[8,1152]{1,0:T(8,128)}, f32[8,1152]{1,0:T(8,128)}) async-done(((f32[8,1152]{1,0:T(8,128)}, f32[8,1152]{1,0:T(8,128)}), (f32[8,1152]{1,0:T(8,128)}, f32[8,1152]{1,0:T(8,128)})) %all-reduce.9.cloned.1.call-update) | async-done | bytes 73744
  70.9 1.4 dynamic-slice_bitcast_fusion
  72.9 136.9 %all-reduce.7.cloned.1.call-done = (f32[384,384]{1,0:T(8,128)}, f32[2,256,256]{2,1,0:T(8,128)}, f32[2,128,128]{2,1,0:T(8,128)}) async-done(((f32[384,384]{1,0:T(8,128)}, f32[2,256,256]{2,1,0:T(8,128)}, f32[2,128,128]{2,1,0:T(8,128)}), (f32[384,384]{1,0:T(8,128)}, f32[2,256,256]{2,1,0:T(8,128)}, f32[2,128,128]{2,1,0:T(8,128)})) %all-reduce.7.cloned.1.call-update) | async-done | bytes 1245200 | tf_op jit(solution)/shard_map/psum | solution.py:152
  209.9 1.8 dynamic-slice_multiply_fusion
  (167 shorter events, 30.3 us)
Async XLA Ops:
  7.2 18.7 %copy-start = (f32[384,384]{1,0:T(8,128)S(1)}, f32[384,384]{1,0:T(8,128)}, u32[]{:S(2)}) copy-start(f32[384,384]{1,0:T(8,128)} %param.12) | copy-start | bytes 1769476
  7.2 63.8 %all-reduce.9.cloned.1.call-start = ((), (), s32[]{:S(2)}) async-start(), calls=%async_computation.1 | async-start | bytes 147456
  21.7 1.2 copy-start.1
  21.8 1.9 copy-start.15
  21.8 1.9 copy-start.17
  21.8 3.0 %copy-start.11 = (f32[128,128]{1,0:T(8,128)}, f32[128,128]{1,0:T(8,128)S(1)}, u32[]{:S(2)}) copy-start(f32[128,128]{1,0:T(8,128)S(1)} %get-tuple-element.11) | copy-start | bytes 196612
  21.8 3.0 %copy-start.13 = (f32[128,128]{1,0:T(8,128)}, f32[128,128]{1,0:T(8,128)S(1)}, u32[]{:S(2)}) copy-start(f32[128,128]{1,0:T(8,128)S(1)} %get-tuple-element.29) | copy-start | bytes 196612
  21.8 4.0 %copy-start.23 = (f32[128,128]{1,0:T(8,128)}, f32[128,128]{1,0:T(8,128)S(1)}, u32[]{:S(2)}) copy-start(f32[128,128]{1,0:T(8,128)S(1)} %get-tuple-element.10) | copy-start | bytes 196612
  21.9 4.0 %copy-start.25 = (f32[128,128]{1,0:T(8,128)}, f32[128,128]{1,0:T(8,128)S(1)}, u32[]{:S(2)}) copy-start(f32[128,128]{1,0:T(8,128)S(1)} %get-tuple-element.30) | copy-start | bytes 196612
  33.5 1.0 copy-start.3
  34.5 1.1 copy-start.36
  35.6 1.4 copy-start.2
  35.9 1.2 copy-start.35
  35.9 1.2 copy-start.39
  37.5 1.0 copy-start.5
  39.5 2.4 %copy-start.29 = (f32[128,1,128]{2,1,0:T(1,128)}, f32[128,1,128]{2,1,0:T(1,128)S(1)}, u32[]{:S(2)}) copy-start(f32[128,1,128]{2,1,0:T(1,128)S(1)} %slice.204) | copy-start | bytes 196612
  40.5 1.4 copy-start.31
  40.5 2.0 copy-start.19
  41.0 1.5 copy-start.21
  50.5 159.4 %all-reduce.7.cloned.1.call-start = ((), (), s32[]{:S(2)}) async-start(), calls=%async_computation | async-start | bytes 2490368 | tf_op jit(solution)/shard_map/psum | solution.py:152
  52.8 1.0 copy-start.34
  70.9 1.4 copy-start.43
  209.9 1.8 copy-start.38
  211.6 1.0 copy-start.40
  (25 other events, 21.1 us)
Sparse Core Ops, SparseCore 0:
  50.6 20.3 all-reduce.8
  77.3 132.5 all-reduce.6
where the time goes:
time: 221 us; the launch traced here: 220 us
  waiting for transfers between devices  147 us (67%)
  matrix products  23.2 us (10%)
  local copies, waits for them, and re-layouts  21.7 us (10%)
  between operations  16.2 us (7%)
  other arithmetic  7.55 us (3%)
  blocking collectives  3.96 us (2%)
    psum x1, waiting for transfers between devices, local(): lax.psum((zero_term, one_term, two_term), ('dp', 'edge'))  137 us
    dot_general x22, matrix products, exact_dot(): jnp.dot(left, right, precision=PRECISE, preferred_element_type=jnp.float32)  10.6 us
    unnamed x3, waiting for transfers between devices  10.3 us
    unnamed x103, local copies, waits for them, and re-layouts  9.85 us
  transfers between devices with their start and end apart: 2, of which 2 were waited for; matrix products, arithmetic and copies ran while one was open for 4% of the time, Pallas kernels for 0%

commit v1 on v0

v1 whole, which is shorter than its diff:
```python
import functools
import math

import jax
import jax.numpy as jnp
from jax import lax
from jax.experimental import pallas as pl
from jax.experimental.pallas import tpu as pltpu
from jax.sharding import PartitionSpec as P

NEIGH = 32
PLACE = (0, 2, 6, 3, 7, 1, 5, 8, 4)
SPOT = tuple(PLACE.index(k) for k in range(9))
MESH = pl.DeviceIdType.MESH
F32 = jnp.float32
B16 = jnp.bfloat16


def digits(count):
    steps = []
    stride = 1
    while stride < count:
        left = count // stride
        radix = 2 if len(steps) < 2 or left < 4 else 4
        steps.append((stride, radix))
        stride *= radix
    assert stride == count
    return steps


def split(x):
    hi = x.astype(B16)
    return hi, (x - hi.astype(F32)).astype(B16)


def dot(a, b, dims=((1,), (0,))):
    return lax.dot_general(a, b, (dims, ((), ())), preferred_element_type=F32)


def dot3(a, b, dims=((1,), (0,))):
    return dot(a[0], b[0], dims) + dot(a[0], b[1], dims) + dot(a[1], b[0], dims)


def plan(dp, shards, ch):
    rz, r1, r2 = 3 * ch // shards, 2 * ch // shards, ch // shards
    valid = (3 * rz + r2, 4 * r1 + r2)
    unit = 8 * dp
    padded = tuple(-(-v // unit) * unit for v in valid)
    steps = digits(dp)
    ahead = list(range(len(steps)))
    swapped = ahead[:2][::-1] + ahead[2:]
    pieces = []
    offset = 0
    for half, rows in enumerate(padded):
        units = rows // unit
        first = (units + 1) // 2
        orders = (ahead, swapped) if half == 0 else (swapped, ahead)
        for size, order in zip((first, units - first), orders):
            if size:
                pieces.append((half, offset, size * unit, order))
                offset += size * unit
    return (rz, r1, r2), valid, padded, steps, pieces


def kernel(
    dp, shards, laid,
    feat_ref, cot_ref, src_ref, tgt_ref, counts_ref, wig_ref, rad_ref, w0_hbm, w1_hbm, w2_hbm,
    agg_ref, fg_ref, g0_ref, g1_ref, g2_ref,
    w0_f, w1_f, w2_f, w0_s, w1_s, w2_s,
    feats, cots, efeat, ecot, wig_t, wb, rot, gmx, mixed, rot_t3, g3,
    esend, erecv, acc, gat, rbuf,
    aggs, aggr, fgs, fgr,
    wsem, fsend, frecv, esnd, ercv, psend, precv, asend, arecv,
):
    (rz, r1, r2), valid, padded, steps, pieces = laid
    edges, ch = rad_ref.shape[1], rad_ref.shape[2]
    atom_dev = feat_ref.shape[1]
    atoms = atom_dev * shards
    apad = -(-atoms // 16) * 16
    wide = 9 * ch
    me_d, me_e = lax.axis_index("dp"), lax.axis_index("edge")
    half_off = (0, padded[0])
    z0, p1, n1, p2, n2 = 0, 3 * ch, 5 * ch, 7 * ch, 8 * ch

    def peer_edge(k):
        return lax.rem(me_e + k, shards)

    def digit(step):
        stride, radix = steps[step]
        return lax.rem(me_d // stride, radix)

    def partner(step, k):
        stride, radix = steps[step]
        mine = digit(step)
        other = lax.rem(mine + k, radix)
        return other, me_d + (other - mine) * stride

    barrier = pltpu.get_barrier_semaphore()
    greeted = 0
    for k in range(1, shards):
        pl.semaphore_signal(barrier, inc=1, device_id=(me_d, peer_edge(k)), device_id_type=MESH)
        greeted += 1
    for step in range(len(steps)):
        for k in range(1, steps[step][1]):
            pl.semaphore_signal(
                barrier, inc=1, device_id=(partner(step, k)[1], me_e), device_id_type=MESH
            )
            greeted += 1

    loads = [
        pltpu.make_async_copy(src, dst, wsem.at[i])
        for i, (src, dst) in enumerate(((w0_hbm, w0_f), (w1_hbm, w1_f), (w2_hbm, w2_f)))
    ]
    for load in loads:
        load.start()

    count = counts_ref[0, 0]
    atom_ids = lax.broadcasted_iota(jnp.int32, (apad, edges), 0)
    slots = lax.broadcasted_iota(jnp.int32, (apad, edges), 1)
    src_hot = jnp.where(atom_ids == src_ref[...], 1.0, 0.0).astype(F32)
    tgt_hot = jnp.where((atom_ids == tgt_ref[...]) & (slots < count), 1.0, 0.0).astype(F32)
    src_cols = jnp.concatenate([src_hot, src_hot], axis=0).T.astype(B16)
    tgt_cols = jnp.concatenate([tgt_hot, tgt_hot], axis=0).T.astype(B16)
    src_rows = jnp.concatenate([src_hot, src_hot], axis=1).astype(B16)
    tgt_rows = jnp.concatenate([tgt_hot, tgt_hot], axis=1).astype(B16)
    wig = jnp.concatenate([wig_ref[0], jnp.zeros((ch - 34, edges), F32)], axis=0)
    wig_t[...] = wig.T
    for half in range(2):
        spare = padded[half] - valid[half]
        if spare:
            acc[half_off[half] + valid[half] : half_off[half] + padded[half], :] = jnp.zeros(
                (spare, ch), F32
            )

    pl.semaphore_wait(barrier, greeted)

    copies = []
    for k in range(1, shards):
        for j, (mine, gathered) in enumerate(((feat_ref, feats), (cot_ref, cots))):
            copy = pltpu.make_async_remote_copy(
                src_ref=mine.at[0],
                dst_ref=gathered.at[me_e],
                send_sem=fsend.at[2 * (k - 1) + j],
                recv_sem=frecv.at[2 * (k - 1) + j],
                device_id=(me_d, peer_edge(k)),
                device_id_type=MESH,
            )
            copy.start()
            copies.append(copy)
    feats[me_e] = feat_ref[0]
    cots[me_e] = cot_ref[0]

    def spread(i, carry):
        rows = pl.ds(pl.multiple_of(i * 8, 8), 8)
        cols = wig_t[rows, :]
        for k in range(34):
            wb[k, rows, :] = jnp.broadcast_to(cols[:, k : k + 1], (8, ch))
        return carry

    lax.fori_loop(0, edges // 8, spread, 0)

    for copy in copies:
        copy.wait()

    def stacked(gathered, factor):
        parts = [gathered[s] for s in range(shards)]
        if apad > atoms:
            parts.append(jnp.zeros((apad - atoms, wide), F32))
        whole = jnp.concatenate(parts, axis=0) * factor
        hi = whole.astype(B16).astype(F32)
        return jnp.concatenate([hi, whole - hi], axis=0).astype(B16)

    norm = 1.0 / math.sqrt(NEIGH)
    efeat[...] = dot(src_cols, stacked(feats, 1.0))
    ecot[...] = dot(tgt_cols, stacked(cots, norm))

    def turn(w, x, inverse):
        out = [x[0]]
        for first, size, base in ((1, 3, 0), (4, 5, 9)):
            for i in range(size):
                total = None
                for j in range(size):
                    entry = base + (size * j + i if inverse else size * i + j)
                    term = w[entry] * x[first + j]
                    total = term if total is None else total + term
                out.append(total)
        return out

    def rotate_in(i, carry):
        rows = pl.ds(pl.multiple_of(i * 8, 8), 8)
        w = [wb[k, rows, :] for k in range(34)]
        radial = rad_ref[0, rows, :]
        x = [efeat[rows, k * ch : (k + 1) * ch] * radial for k in range(9)]
        for k, value in enumerate(turn(w, x, False)):
            rot[rows, SPOT[k] * ch : (SPOT[k] + 1) * ch] = value
        x = [ecot[rows, k * ch : (k + 1) * ch] for k in range(9)]
        for k, value in enumerate(turn(w, x, False)):
            gmx[rows, SPOT[k] * ch : (SPOT[k] + 1) * ch] = value
        return carry

    lax.fori_loop(0, edges // 8, rotate_in, 0)

    for b in range(9):
        cols = slice(b * ch, (b + 1) * ch)
        hi, lo = split(rot[:, cols].T)
        rot_t3[cols, 0:edges] = hi
        rot_t3[cols, edges : 2 * edges] = hi
        rot_t3[cols, 2 * edges :] = lo
        hi, lo = split(gmx[:, cols])
        g3[0:edges, cols] = hi
        g3[edges : 2 * edges, cols] = lo
        g3[2 * edges :, cols] = hi

    def lhs(start, size, owner):
        return rot_t3[pl.ds(pl.multiple_of(start + owner * size, 16), size), :]

    def share_a(owner, out):
        zero = dot(lhs(z0, rz, owner), g3[:, z0:p1])
        for b in range(3):
            out[b * rz : (b + 1) * rz, :] = zero[:, b * ch : (b + 1) * ch]
        out[3 * rz : 3 * rz + r2, :] = dot(lhs(p2, r2, owner), g3[:, p2:n2]) + dot(
            lhs(n2, r2, owner), g3[:, n2:]
        )

    def share_b(owner, out):
        plus, minus = lhs(p1, r1, owner), lhs(n1, r1, owner)
        gp, gn = g3[:, p1:n1], g3[:, n1:p2]
        real = dot(plus, gp) + dot(minus, gn)
        imag = dot(plus, gn) - dot(minus, gp)
        for b in range(2):
            out[b * r1 : (b + 1) * r1, :] = real[:, b * ch : (b + 1) * ch]
            out[(2 + b) * r1 : (3 + b) * r1, :] = imag[:, b * ch : (b + 1) * ch]
        out[4 * r1 : 4 * r1 + r2, :] = dot(lhs(p2, r2, owner), g3[:, n2:]) - dot(
            lhs(n2, r2, owner), g3[:, p2:n2]
        )

    shares = (share_a, share_b)
    ecopies = [[], []]
    for half in range(2):
        for k in range(1, shards):
            span = pl.ds(half_off[half], valid[half])
            shares[half](peer_edge(k), esend.at[k - 1, span])
            copy = pltpu.make_async_remote_copy(
                src_ref=esend.at[k - 1, span],
                dst_ref=erecv.at[k - 1, span],
                send_sem=esnd.at[2 * (k - 1) + half],
                recv_sem=ercv.at[2 * (k - 1) + half],
                device_id=(me_d, peer_edge(k)),
                device_id_type=MESH,
            )
            copy.start()
            ecopies[half].append(copy)

    grad_scale = 1.0 / math.sqrt(dp * shards * edges)
    slots_used = [0, 0]
    jobs = []

    class Piece:
        pass

    for half, offset, length, order in pieces:
        piece = Piece()
        piece.half, piece.order, piece.at, piece.len = half, order, offset, length
        piece.base = jnp.int32(0) + offset
        piece.trail = []
        piece.pending = None
        piece.every = []
        jobs.append(piece)

    def send_to(src, dst, target):
        sem = slots_used[0]
        slots_used[0] += 1
        copy = pltpu.make_async_remote_copy(
            src_ref=src, dst_ref=dst, send_sem=psend.at[sem], recv_sem=precv.at[sem],
            device_id=(target, me_e), device_id_type=MESH,
        )
        copy.start()
        return copy

    def start_scatter(piece, n):
        step = piece.order[n]
        part = piece.len // steps[step][1]
        piece.pending = []
        for k in range(1, steps[step][1]):
            other, target = partner(step, k)
            begin = pl.multiple_of(piece.base + other * part, 8)
            slot = pl.ds(slots_used[1], part)
            slots_used[1] += part
            copy = send_to(acc.at[pl.ds(begin, part)], rbuf.at[slot], target)
            piece.pending.append((copy, slot))

    def end_scatter(piece, n):
        step = piece.order[n]
        part = piece.len // steps[step][1]
        piece.trail.append((piece.base, piece.len))
        piece.base = piece.base + digit(step) * part
        piece.len = part
        own = pl.ds(pl.multiple_of(piece.base, 8), part)
        total = acc[own, :]
        for copy, slot in piece.pending:
            copy.wait_recv()
            piece.every.append(copy)
            total = total + rbuf[slot, :]
        if n == len(steps) - 1:
            gat[own, :] = total * grad_scale
        else:
            acc[own, :] = total

    def start_gather(piece, n):
        step = piece.order[n]
        own = pl.ds(pl.multiple_of(piece.base, 8), piece.len)
        piece.pending = [
            send_to(gat.at[own], gat.at[own], partner(step, k)[1])
            for k in range(1, steps[step][1])
        ]

    def end_gather(piece, n):
        for copy in piece.pending:
            copy.wait_recv()
            piece.every.append(copy)
        piece.base, piece.len = piece.trail.pop()

    last = len(steps) - 1
    if dp == 1:
        jobs = []

    for half in range(2):
        span = pl.ds(half_off[half], valid[half])
        shares[half](me_e, acc.at[span])
        total = acc[span, :]
        for k, copy in enumerate(ecopies[half]):
            copy.wait_recv()
            total = total + erecv[k, span, :]
        acc[span, :] = total
        for piece in jobs:
            if piece.half == half:
                start_scatter(piece, 0)

    eye = ((1,), (0,))
    flip = ((1,), (1,))

    def mix(hi, lo, out, sign, dims):
        zero = dot3((hi[:, z0:p1], lo[:, z0:p1]), (w0_s[0], w0_s[1]), dims)
        out[:, z0:p1] = zero
        for begin, middle, end, weights in ((p1, n1, p2, w1_s), (p2, n2, wide, w2_s)):
            pair = tuple(
                jnp.concatenate([v[:, begin:middle], v[:, middle:end]], axis=0) for v in (hi, lo)
            )
            real = dot3(pair, (weights[0, 0], weights[1, 0]), dims)
            imag = dot3(pair, (weights[0, 1], weights[1, 1]), dims)
            if sign > 0:
                out[:, begin:middle] = real[:edges] - imag[edges:]
                out[:, middle:end] = real[edges:] + imag[:edges]
            else:
                out[:, begin:middle] = real[:edges] + imag[edges:]
                out[:, middle:end] = real[edges:] - imag[:edges]

    def rotate_out(dest, use_radial):
        def body(i, carry):
            rows = pl.ds(pl.multiple_of(i * 8, 8), 8)
            w = [wb[k, rows, :] for k in range(34)]
            x = [mixed[rows, SPOT[k] * ch : (SPOT[k] + 1) * ch] for k in range(9)]
            for k, value in enumerate(turn(w, x, True)):
                if use_radial:
                    value = value * rad_ref[0, rows, :]
                dest[rows, k * ch : (k + 1) * ch] = value
            return carry

        lax.fori_loop(0, edges // 8, body, 0)

    def collect(hot, values, factor, sent, received, sem):
        hi, lo = split(values[...])
        total = dot(hot, jnp.concatenate([hi, lo], axis=0)) * factor
        for s in range(shards):
            sent[s] = total[s * atom_dev : (s + 1) * atom_dev]
        started = []
        for k in range(1, shards):
            copy = pltpu.make_async_remote_copy(
                src_ref=sent.at[peer_edge(k)],
                dst_ref=received.at[k - 1],
                send_sem=asend.at[2 * (k - 1) + sem],
                recv_sem=arecv.at[2 * (k - 1) + sem],
                device_id=(me_d, peer_edge(k)),
                device_id_type=MESH,
            )
            copy.start()
            started.append(copy)
        return started

    tail = {}

    def forward_mix():
        for load in loads:
            load.wait()
        hi, lo = split(w0_f[...])
        w0_s[0], w0_s[1] = hi, lo
        hi, lo = split(w1_f[...])
        w1_s[0], w1_s[1] = hi, lo
        hi, lo = split(w2_f[...])
        w2_s[0], w2_s[1] = hi, lo
        hi, lo = split(rot[...])
        mix(hi, lo, mixed, 1, eye)

    def forward_rest():
        rotate_out(efeat, False)
        tail["agg"] = collect(tgt_rows, efeat, norm, aggs, aggr, 0)

    def backward_mix():
        mix(g3[0:edges, :], g3[edges : 2 * edges, :], mixed, -1, flip)

    def backward_rest():
        rotate_out(ecot, True)
        tail["fg"] = collect(src_rows, ecot, 1.0, fgs, fgr, 1)

    def finish_rows():
        for name, out, sent, received in (("agg", agg_ref, aggs, aggr), ("fg", fg_ref, fgs, fgr)):
            total = sent[me_e]
            for k, copy in enumerate(tail[name]):
                copy.wait()
                total = total + received[k]
            out[0] = total

    work = [forward_mix, forward_rest, backward_mix, backward_rest, finish_rows]

    for n in range(len(steps)):
        if work:
            work.pop(0)()
        for piece in jobs:
            end_scatter(piece, n)
            if n < last:
                start_scatter(piece, n + 1)
            else:
                start_gather(piece, n)
    for n in reversed(range(len(steps))):
        if work:
            work.pop(0)()
        for piece in jobs:
            end_gather(piece, n)
            if n > 0:
                start_gather(piece, n - 1)
    while work:
        work.pop(0)()
    for half in range(2):
        for copy in ecopies[half]:
            copy.wait_send()
    for piece in jobs:
        for copy in piece.every:
            copy.wait_send()

    source = gat if dp > 1 else acc
    factor = 1.0 if dp > 1 else grad_scale

    def block(begin, size):
        value = source[begin : begin + size, :]
        return value if dp > 1 else value * factor

    for b in range(3):
        g0_ref[:, b * ch : (b + 1) * ch] = block(b * rz, rz)
    g2_ref[0] = block(3 * rz, r2)
    for part in range(2):
        for b in range(2):
            g1_ref[part, :, b * ch : (b + 1) * ch] = block(half_off[1] + (2 * part + b) * r1, r1)
    g2_ref[1] = block(half_off[1] + 4 * r1, r2)


def local(dp, shards, node_feat, cotangent, w_zero, w_one, w_two, edge_src, edge_tgt, counts, wigner, radial):
    atom_dev = node_feat.shape[1]
    edges, ch = radial.shape[1], radial.shape[2]
    wide = 9 * ch
    laid = plan(dp, shards, ch)
    (rz, r1, r2), valid, padded, steps, pieces = laid
    rows = sum(padded)
    copies = 0
    landing = 0
    for _, _, length, order in pieces:
        for n in order:
            radix = steps[n][1]
            copies += 2 * (radix - 1)
            length //= radix
            landing += length * (radix - 1)
    peers = max(shards - 1, 1)
    vmem = pl.BlockSpec(memory_space=pltpu.VMEM)
    smem = pl.BlockSpec(memory_space=pltpu.SMEM)
    anywhere = pl.BlockSpec(memory_space=pl.ANY)
    dma = pltpu.SemaphoreType.DMA
    return pl.pallas_call(
        functools.partial(kernel, dp, shards, laid),
        out_shape=(
            jax.ShapeDtypeStruct((1, atom_dev, wide), F32),
            jax.ShapeDtypeStruct((1, atom_dev, wide), F32),
            jax.ShapeDtypeStruct((rz, 3 * ch), F32),
            jax.ShapeDtypeStruct((2, r1, 2 * ch), F32),
            jax.ShapeDtypeStruct((2, r2, ch), F32),
        ),
        in_specs=[vmem, vmem, vmem, vmem, smem, vmem, vmem, anywhere, anywhere, anywhere],
        out_specs=(vmem,) * 5,
        scratch_shapes=[
            pltpu.VMEM(w_zero.shape, F32),
            pltpu.VMEM(w_one.shape, F32),
            pltpu.VMEM(w_two.shape, F32),
            pltpu.VMEM((2,) + w_zero.shape, B16),
            pltpu.VMEM((2,) + w_one.shape, B16),
            pltpu.VMEM((2,) + w_two.shape, B16),
            pltpu.VMEM((shards, atom_dev, wide), F32),
            pltpu.VMEM((shards, atom_dev, wide), F32),
            pltpu.VMEM((edges, wide), F32),
            pltpu.VMEM((edges, wide), F32),
            pltpu.VMEM((edges, ch), F32),
            pltpu.VMEM((34, edges, ch), F32),
            pltpu.VMEM((edges, wide), F32),
            pltpu.VMEM((edges, wide), F32),
            pltpu.VMEM((edges, wide), F32),
            pltpu.VMEM((wide, 3 * edges), B16),
            pltpu.VMEM((3 * edges, wide), B16),
            pltpu.VMEM((peers, rows, ch), F32),
            pltpu.VMEM((peers, rows, ch), F32),
            pltpu.VMEM((rows, ch), F32),
            pltpu.VMEM((rows, ch), F32),
            pltpu.VMEM((max(landing, 8), ch), F32),
            pltpu.VMEM((shards, atom_dev, wide), F32),
            pltpu.VMEM((peers, atom_dev, wide), F32),
            pltpu.VMEM((shards, atom_dev, wide), F32),
            pltpu.VMEM((peers, atom_dev, wide), F32),
            dma((3,)),
            dma((2 * peers,)),
            dma((2 * peers,)),
            dma((2 * peers,)),
            dma((2 * peers,)),
            dma((max(copies, 1),)),
            dma((max(copies, 1),)),
            dma((2 * peers,)),
            dma((2 * peers,)),
        ],
        compiler_params=pltpu.CompilerParams(
            collective_id=0, has_side_effects=True, vmem_limit_bytes=40 * 1024 * 1024
        ),
    )(node_feat, cotangent, edge_src, edge_tgt, counts, wigner, radial, w_zero, w_one, w_two)


def solution(mesh):
    placed = (
        P("dp", "edge", None),
        P("dp", "edge", None),
        P(),
        P(),
        P(),
        P("dp", "edge"),
        P("dp", "edge"),
        P("dp", "edge"),
        P("dp", None, "edge"),
        P("dp", "edge", None),
    )
    return jax.shard_map(
        functools.partial(local, mesh.shape["dp"], mesh.shape["edge"]),
        mesh=mesh,
        in_specs=placed,
        out_specs=(
            P("dp", "edge", None),
            P("dp", "edge", None),
            P("edge", None),
            P(None, "edge", None),
            P(None, "edge", None),
        ),
        check_vma=False,
    )
```

time: 221 us -> 44.2 us (0.20)
  waiting for transfers between devices: 147 us -> 0 us
  Pallas kernels: 0 us -> 34.7 us
  matrix products: 23.2 us -> 0 us
  between operations: 16.2 us -> 1.35 us
  local copies, waits for them, and re-layouts: 21.7 us -> 7.86 us
  other arithmetic: 7.55 us -> 0 us
  blocking collectives: 3.96 us -> 0 us
    psum x1 -> x0, waiting for transfers between devices: 137 us -> none  [local(): lax.psum((zero_term, one_term, two_term), ('dp', 'edge'))]
    pallas_call x0 -> x1, Pallas kernels: none -> 34.7 us  [local(): pl.pallas_call(functools.partial(kernel, dp, shards, laid), out_shape=(ja...]
    dot_general x39 -> x0, matrix products: 23.2 us -> none  [the longest x22 10.6 us: exact_dot(): jnp.dot(left, right, precision=PRECISE, preferred_element_type=jnp.float32)]
    unnamed x3 -> x0, waiting for transfers between devices: 10.3 us -> none
    mul x6 -> x0, other arithmetic: 4.79 us -> none  [the longest x1 1.75 us: local(): rows_zero * grad_scale]
    reshape x8 -> x0, local copies, waits for them, and re-layouts: 4.13 us -> none  [the longest x3 1.73 us: rotate(): order_one = wigner_cols[0:9].reshape(3, 3, edge_count)]
    all_gather x2 -> x0, blocking collectives: 3.96 us -> none  [the longest x1 2.01 us: local(): lax.all_gather(feat_rows, 'edge', axis=0, tiled=True)]
    slice x6 -> x0, local copies, waits for them, and re-layouts: 2.86 us -> none  [the longest x1 0.8 us: rotate(): order_two = wigner_cols[9:34].reshape(5, 5, edge_count)]
  transfers between devices with their start and end apart: 2 -> 0, of which waited for: 2 -> 0; matrix products, arithmetic and copies ran while one was open for 4% -> 0% of each run, Pallas kernels for 0% -> 0%
where the time goes in v1:
time: 44.2 us; the launch traced here: 43.9 us
  Pallas kernels  34.7 us (79%)
  local copies, waits for them, and re-layouts  7.86 us (18%)
  between operations  1.35 us (3%)
    pallas_call x1, Pallas kernels, local(): pl.pallas_call(functools.partial(kernel, dp, shards, laid), out_shape=(ja...  34.7 us
    unnamed x22, local copies, waits for them, and re-layouts  7.86 us

profile of v1, /device:TPU:0, one launch (start us, length us, event | category | flops | bytes accessed | tf_op | source)
XLA Modules:
  0.0 43.9 jit_solution(2998577286358233873)
XLA Ops:
  1.3 0.0 copy-start.4
  1.3 0.0 copy-start.5
  1.3 0.0 copy-start.6
  1.3 0.0 copy-start.7
  1.3 0.7 %copy.15.wig_ref = f32[1,34,128]{2,1,0:T(8,128)S(1)} copy(f32[1,34,128]{2,0,1:T(1,128)} %param.18) | data formatting | bytes 34816 | tf_op args[8]
  2.1 0.0 copy-done.4
  2.1 0.0 copy-done.5
  2.1 0.0 copy-done.6
  2.1 0.0 copy-done.7
  2.1 0.0 copy-start
  2.1 1.1 %copy-done = f32[384,384]{1,0:T(8,128)S(1)} copy-done((f32[384,384]{1,0:T(8,128)S(1)}, f32[384,384]{1,0:T(8,128)}, u32[]{:S(2)}) %copy-start) | copy-done | bytes 589848
  3.2 0.0 copy-start.1
  3.2 1.0 %copy-done.1 = f32[2,256,256]{2,1,0:T(8,128)S(1)} copy-done((f32[2,256,256]{2,1,0:T(8,128)S(1)}, f32[2,256,256]{2,1,0:T(8,128)}, u32[]{:S(2)}) %copy-start.1) | copy-done | bytes 524312
  4.2 0.0 copy-start.2
  4.2 0.9 %copy-done.2 = f32[2,128,128]{2,1,0:T(8,128)S(1)} copy-done((f32[2,128,128]{2,1,0:T(8,128)S(1)}, f32[2,128,128]{2,1,0:T(8,128)}, u32[]{:S(2)}) %copy-start.2) | copy-done | bytes 131096
  5.1 0.0 copy-start.3
  5.1 0.8 %copy-done.3 = f32[1,128,128]{2,1,0:T(8,128)S(1)} copy-done((f32[1,128,128]{2,1,0:T(8,128)S(1)}, f32[1,128,128]{2,1,0:T(8,128)}, u32[]{:S(2)}) %copy-start.3) | copy-done | bytes 65560
  5.9 34.7 %shard_map.137 = (f32[1,4,1152]{2,1,0:T(4,128)S(1)}, f32[1,4,1152]{2,1,0:T(4,128)S(1)}, f32[192,384]{1,0:T(8,128)S(1)}, f32[2,128,256]{2,1,0:T(8,128)S(1)}, f32[2,64,128]{2,1,0:T(8,128)S(1)}) custom-call(f32[1,4,1152]{2,1,0:T(4,128)S(1)} %copy-done.4, f32[1,4,1152]{2,1,0:T(4,128)S(1)} %copy-done.5, s32[1,128]{1,0:T(1,128)S(1)} %copy-done.6, ...), custom_call_target="tpu_custom_call" | custom-call | tf_op jit(solution)/shard_map/pallas_call | solution.py:486
  40.6 0.6 %copy.22 = f32[1,4,1152]{2,1,0:T(4,128)} copy(f32[1,4,1152]{2,1,0:T(4,128)S(1)} %get-tuple-element.10) | data formatting | bytes 36864
  41.2 0.6 %copy.23 = f32[1,4,1152]{2,1,0:T(4,128)} copy(f32[1,4,1152]{2,1,0:T(4,128)S(1)} %get-tuple-element.11) | data formatting | bytes 36864
  41.8 0.7 %copy.24 = f32[192,384]{1,0:T(8,128)} copy(f32[192,384]{1,0:T(8,128)S(1)} %get-tuple-element.12) | data formatting | bytes 589824
  42.5 0.7 %copy.25 = f32[2,128,256]{2,1,0:T(8,128)} copy(f32[2,128,256]{2,1,0:T(8,128)S(1)} %get-tuple-element.13) | data formatting | bytes 524288
  43.2 0.6 %copy.26 = f32[2,64,128]{2,1,0:T(8,128)} copy(f32[2,64,128]{2,1,0:T(8,128)S(1)} %get-tuple-element.14) | data formatting | bytes 131072
Async XLA Ops:
  1.3 0.8 %copy-start.4 = (f32[1,4,1152]{2,1,0:T(4,128)S(1)}, f32[1,4,1152]{2,1,0:T(4,128)}, u32[]{:S(2)}) copy-start(f32[1,4,1152]{2,1,0:T(4,128)} %feat_ref.1) | copy-start | bytes 55300
  1.3 0.8 %copy-start.5 = (f32[1,4,1152]{2,1,0:T(4,128)S(1)}, f32[1,4,1152]{2,1,0:T(4,128)}, u32[]{:S(2)}) copy-start(f32[1,4,1152]{2,1,0:T(4,128)} %cot_ref.1) | copy-start | bytes 55300
  1.3 0.8 %copy-start.6 = (s32[1,128]{1,0:T(1,128)S(1)}, s32[1,128]{1,0:T(1,128)}, u32[]{:S(2)}) copy-start(s32[1,128]{1,0:T(1,128)} %src_ref.1) | copy-start | bytes 1540
  1.3 0.8 %copy-start.7 = (s32[1,128]{1,0:T(1,128)S(1)}, s32[1,128]{1,0:T(1,128)}, u32[]{:S(2)}) copy-start(s32[1,128]{1,0:T(1,128)} %tgt_ref.1) | copy-start | bytes 1540
  2.1 1.1 %copy-start = (f32[384,384]{1,0:T(8,128)S(1)}, f32[384,384]{1,0:T(8,128)}, u32[]{:S(2)}) copy-start(f32[384,384]{1,0:T(8,128)} %w0_hbm.1) | copy-start | bytes 1769476
  3.2 1.0 %copy-start.1 = (f32[2,256,256]{2,1,0:T(8,128)S(1)}, f32[2,256,256]{2,1,0:T(8,128)}, u32[]{:S(2)}) copy-start(f32[2,256,256]{2,1,0:T(8,128)} %w1_hbm.1) | copy-start | bytes 1572868
  4.2 0.9 %copy-start.2 = (f32[2,128,128]{2,1,0:T(8,128)S(1)}, f32[2,128,128]{2,1,0:T(8,128)}, u32[]{:S(2)}) copy-start(f32[2,128,128]{2,1,0:T(8,128)} %w2_hbm.1) | copy-start | bytes 393220
  5.1 0.8 %copy-start.3 = (f32[1,128,128]{2,1,0:T(8,128)S(1)}, f32[1,128,128]{2,1,0:T(8,128)}, u32[]{:S(2)}) copy-start(f32[1,128,128]{2,1,0:T(8,128)} %rad_ref.1) | copy-start | bytes 196612
